TPU v7x, 32 devices: a whole 2x2x4 slice. The times are simulated.
32 devices in a mesh: group: 2 (over y), dp: 4 (over x, core), tensor: 4 (over z).
Axes of the slice: x: 2, y: 2, z: 4, core: 2. Of those that a mesh axis runs over, the one named last changes fastest.
Arguments:
- tokens: bfloat16 [8192, 1024], P(('group', 'dp')), parts along dimension 0, may hold values from -6 to 6
- past_states: float32 [256, 8, 128, 128], P(('group', 'dp'), 'tensor'), parts along dimension 0, may hold values from -3 to 3
- attn_weights: bfloat16 [5, 1024, 1024], P(None, 'dp', 'tensor'), may hold values from -0.1875 to 0.1875
- ffn_weights: bfloat16 [2, 1024, 4096], P(None, 'dp', 'tensor'), may hold values from -0.1875 to 0.1875
- norm_gains: float32 [2, 1024], replicated, may hold values from 0.1 to 1.9
- head_rates: float32 [8], replicated, may hold values from 0.004 to 0.15
- end_lengths: int32 [256], P(('group', 'dp')), parts along dimension 0, may hold values from 1 to 64, as said below
- new_slot: int32 [256], P(('group', 'dp')), parts along dimension 0, may hold values from 0 to 127, as said below
Outputs:
- next_tokens: bfloat16 [8192, 1024], P(('group', 'dp'), 'tensor'), parts along dimension 0
- moved_states: float32 [256, 8, 128, 128], P(('group', 'dp'), 'tensor'), parts along dimension 0
There are 2 independent parts, one for each index of `group`. A program takes and returns all parts, laid end to end along the dimension named above; an argument that names none is the same for every part. Nothing has to cross between parts.
Inputs may be any that keep to these rules, and one draw needn't show every extreme that they name: `end_lengths`: of the sessions in one aligned block of 32 sessions whose end lengths exceed 32, at most 16 have new slots in one aligned block of 32 slots, and some pair of blocks has exactly 16. `new_slot`: A permutation of the 128 slots.
All inputs are finite; a program needn't handle non-finite values.
Results may differ from a plain program's by a relative error of at most 0.018.
Values may be sent and summed in bfloat16 or wider, within the bound.
A program may use at most 64 MiB of HBM per device.

v0:
```python
import functools

import jax
import jax.numpy as jnp
from jax import lax
from jax.experimental import pallas as pl
from jax.experimental.pallas import tpu as pltpu
from jax.sharding import PartitionSpec as P


def pick_kernel(index_ref, keep_ref, values_ref, out_ref):
    def body(at, carry):
        kept = keep_ref[at].astype(jnp.float32)
        out_ref[at] = jnp.where(
            kept > 0, values_ref[index_ref[at]].astype(jnp.float32), 0.0
        ).astype(out_ref.dtype)
        return carry

    lax.fori_loop(0, out_ref.shape[0], body, 0)


def pick(values, index, keep, dtype):
    return pl.pallas_call(
        pick_kernel,
        out_shape=jax.ShapeDtypeStruct(index.shape + values.shape[1:], dtype),
        in_specs=[pl.BlockSpec(memory_space=pltpu.SMEM)] * 2
        + [pl.BlockSpec(memory_space=pltpu.VMEM)],
        out_specs=pl.BlockSpec(memory_space=pltpu.VMEM),
        compiler_params=pltpu.CompilerParams(vmem_limit_bytes=48 * 2**20),
    )(index.astype(jnp.int32), keep.astype(jnp.int32), values)


MESH = pl.DeviceIdType.MESH


def part_of(ref, dim, at, size):
    index = [slice(None)] * len(ref.shape)
    index[dim] = pl.ds(at * size, size)
    return ref.at[tuple(index)]


def exchange_kernel(jobs, axes, *refs):
    count = len(jobs)
    sources, outs = refs[:count], refs[count : 2 * count]
    sems, held = refs[2 * count : 3 * count], refs[3 * count :]
    barrier = pltpu.get_barrier_semaphore()
    greeted = 0
    for axis, size in axes:
        me = lax.axis_index(axis)
        for step in range(1, size):
            pl.semaphore_signal(
                barrier, inc=1, device_id={axis: lax.rem(me + step, size)}, device_id_type=MESH
            )
            greeted += 1
    pl.semaphore_wait(barrier, greeted)
    sizes = dict(axes)
    events, arrivals, started, locals_ = [], [], [], []

    def remote(job_at, number, source, target, axis, device):
        return pltpu.make_async_remote_copy(
            src_ref=source,
            dst_ref=target,
            send_sem=sems[job_at].at[0, number],
            recv_sem=sems[job_at].at[1, number],
            device_id={axis: device},
            device_id_type=MESH,
        )

    def begin(copy):
        copy.start()
        started.append(copy.wait_send)

    def plain(job_at, source, out, axis, dim, kind):
        size = sizes[axis]
        me = lax.axis_index(axis)
        width = source.shape[dim] // (size if kind == "scatter" else 1)
        for step in range(1, size):
            other, origin = lax.rem(me + step, size), lax.rem(me + size - step, size)
            if kind == "scatter":
                block, put = part_of(source, dim, other, width), out.at[me]
                got = out.at[origin]
            else:
                block, put = source, part_of(out, dim, me, width)
                got = part_of(out, dim, origin, width)
            begin(remote(job_at, step, block, put, axis, other))
            arrivals.append(remote(job_at, step, block, got, axis, other).wait_recv)

    def relay(job_at, source, out, axis, dim):
        size, groups = sizes[axis], sizes["group"]
        me, group = lax.axis_index(axis), lax.axis_index("group")
        chips, chip, core = size // 2, me // 2, lax.rem(me, 2)
        sibling = chip * 2 + 1 - core
        width = source.shape[dim]
        turns = relay_turns(width, groups)
        chunk = width // (turns * groups)

        def place(ref, owner, at):
            return part_of(ref, dim, owner * (turns * groups) + at, chunk)

        number = iter(range(1, 1 << 16))
        for turn in range(turns):
            at = turn * groups + group
            for step in range(1, chips):
                other = lax.rem(chip + step, chips) * 2 + core
                origin = lax.rem(chip + chips - step, chips) * 2
                over, down = next(number), next(number)
                begin(remote(job_at, over, place(source, 0, at), place(out, me, at), axis, other))
                here, there = place(out, origin + core, at), place(out, origin + 1 - core, at)
                ways = [next(number) for _ in range(2 * (groups - 1))]

                def arrive(over=over, down=down, here=here, ways=ways):
                    remote(job_at, over, here, here, axis, sibling).wait_recv()
                    for shift in range(1, groups):
                        begin(
                            remote(
                                job_at, ways[shift - 1], here, here, "group",
                                lax.rem(group + shift, groups),
                            )
                        )
                    begin(remote(job_at, down, here, here, axis, sibling))

                events.append(((turn + 1) / turns, arrive))
                arrivals.append(remote(job_at, down, there, there, axis, sibling).wait_recv)
                for shift in range(1, groups):
                    late = turn * groups + lax.rem(group + groups - shift, groups)
                    first, last = ways[shift - 1], ways[groups - 2 + shift]
                    here, there = place(out, origin + core, late), place(out, origin + 1 - core, late)

                    def hand(first=first, last=last, here=here):
                        remote(job_at, first, here, here, axis, sibling).wait_recv()
                        begin(remote(job_at, last, here, here, axis, sibling))

                    events.append(((turn + 2.1) / turns, hand))
                    arrivals.append(remote(job_at, last, there, there, axis, sibling).wait_recv)
        whole = next(number)
        begin(remote(job_at, whole, source, part_of(out, dim, me, width), axis, sibling))
        got = part_of(out, dim, sibling, width)
        arrivals.append(remote(job_at, whole, source, got, axis, sibling).wait_recv)

    def chain(job_at, source, out, axis, dim):
        size = sizes[axis]
        me = lax.axis_index(axis)
        width, rows = source.shape[dim], source.shape[0]
        cuts = CHAIN_CUTS
        for step in range(size):
            for cut in range(cuts):
                across = pl.ds(cut * (rows // cuts), rows // cuts)
                for way, sign in enumerate((1, -1)):
                    origin = me - sign * step
                    held = (origin >= 0) & (origin < size)
                    onward = held & (me + sign >= 0) & (me + sign < size)
                    safe = jnp.clip(origin, 0, size - 1)
                    there = out.at[across, pl.ds(safe * width, width)]
                    block = source.at[across] if step == 0 else there
                    now = 1 + (step * cuts + cut) * 2 + way
                    after = now + 2 * cuts
                    neighbour = jnp.clip(me + sign, 0, size - 1)

                    def act(step=step, now=now, after=after, there=there, block=block, held=held,
                            onward=onward, neighbour=neighbour):
                        if step > 0:
                            pl.when(held)(
                                lambda: remote(job_at, now, there, there, axis, neighbour).wait_recv()
                            )
                        if step < size - 1:
                            copy = remote(job_at, after, block, there, axis, neighbour)
                            pl.when(onward)(lambda: copy.start())
                            started.append(lambda: pl.when(onward)(lambda: copy.wait_send()))

                    if step == 0:
                        act()
                    else:
                        events.append(((step - 1 + (cut + 1) / cuts) / (size - 1), act))

    for job_at, (kind, axis, dim, lead) in enumerate(jobs):
        source, out = sources[job_at], outs[job_at]
        if lead:
            source = source.at[lead[0] : lead[1]] if lead[1] > lead[0] + 1 else source.at[lead[0]]
        me = lax.axis_index(axis)
        if kind == "relay":
            relay(job_at, source, out, axis, dim)
        elif kind == "chain":
            chain(job_at, source, out, axis, dim)
        else:
            plain(job_at, source, out, axis, dim, kind)
        if kind == "scatter":
            block = part_of(source, dim, me, source.shape[dim] // sizes[axis])
            mine = out.at[me]
        else:
            block, mine = source, part_of(out, dim, me, source.shape[dim])
        locals_.append(
            (
                pltpu.make_async_copy(block, held[job_at], sems[job_at].at[0, 0]),
                pltpu.make_async_copy(held[job_at], mine, sems[job_at].at[1, 0]),
            )
        )
    for fetch, _ in locals_:
        fetch.start()
    for fetch, put in locals_:
        fetch.wait()
        put.start()
        arrivals.append(put.wait)
    for _, act in sorted(events, key=lambda event: event[0]):
        act()
    for wait in arrivals:
        wait()
    for wait in started:
        wait()


CHAIN_CUTS = 4


def relay_turns(width, groups):
    return max(1, min(8, width // 16) // groups)


def exchange(mesh_shape, collective_id, *tasks):
    used = [task[2] for task in tasks] + ["group" for task in tasks if task[1] == "relay"]
    axes = tuple((axis, mesh_shape[axis]) for axis in ("group", "dp", "tensor") if axis in used)
    shapes, sems, held = [], [], []
    for values, kind, axis, dim, lead in tasks:
        size = mesh_shape[axis]
        shape = list(values.shape)
        if lead:
            shape = ([lead[1] - lead[0]] if lead[1] > lead[0] + 1 else []) + shape[1:]
        number = size + 1
        if kind == "relay":
            groups = mesh_shape["group"]
            turns = relay_turns(shape[dim], groups)
            number = 2 + turns * (size // 2 - 1) * 2 * groups
        elif kind == "chain":
            number = 1 + 2 * CHAIN_CUTS * size
        if kind == "scatter":
            shape[dim] //= size
            held.append(pltpu.VMEM(tuple(shape), values.dtype))
            shape = [size] + shape
        else:
            held.append(pltpu.VMEM(tuple(shape), values.dtype))
            shape[dim] *= size
        shapes.append(jax.ShapeDtypeStruct(tuple(shape), values.dtype))
        sems.append(pltpu.SemaphoreType.DMA((2, number)))
    sent = sum(values.size * values.dtype.itemsize for values, *_ in tasks)
    return pl.pallas_call(
        functools.partial(exchange_kernel, tuple(task[1:] for task in tasks), axes),
        out_shape=shapes,
        in_specs=[pl.BlockSpec(memory_space=pl.ANY)] * len(tasks),
        out_specs=[pl.BlockSpec(memory_space=pl.ANY)] * len(tasks),
        scratch_shapes=sems + held,
        cost_estimate=pl.CostEstimate(flops=0, bytes_accessed=8 * sent, transcendentals=0),
        compiler_params=pltpu.CompilerParams(
            collective_id=collective_id, has_side_effects=True, vmem_limit_bytes=16 * 2**20
        ),
    )(*(task[0] for task in tasks))


def rms_scale(values, gain_row):
    meansq = jnp.mean(values * values, axis=-1, keepdims=True)
    return (values * lax.rsqrt(meansq + 1e-05) * gain_row).astype(jnp.bfloat16)


def update_state(past_block, key_rows, value_rows, head_decay):
    event_count = key_rows.shape[2]
    position = jnp.arange(event_count).astype(jnp.float32)
    key_scale = key_rows.shape[3] ** (-0.5)
    factor = jnp.exp(-head_decay[:, None] * (event_count - 1.0 - position)[None, :])
    weighted = key_rows.astype(jnp.float32) * key_scale * factor[:, :, None]
    carried = jnp.exp(-head_decay * event_count)[:, None, None] * past_block
    return carried + jnp.einsum(
        "ghjd,ghje->ghde", weighted.astype(jnp.bfloat16), value_rows, preferred_element_type=jnp.float32
    )


def retain_events(query, key_rows, value_rows, past_block, head_decay):
    event_count = query.shape[2]
    position = jnp.arange(event_count).astype(jnp.float32)
    distance = position[:, None] - position[None, :]
    decay = jnp.where(
        distance >= 0, jnp.exp(-head_decay[:, None, None] * jnp.maximum(distance, 0.0)), 0.0
    )
    key_scale = query.shape[3] ** (-0.5)
    scores = (
        jnp.einsum("ghid,ghjd->ghij", query, key_rows, preferred_element_type=jnp.float32)
        * key_scale
    )
    weights_mix = (scores * decay).astype(jnp.bfloat16)
    intra_term = jnp.einsum(
        "ghij,ghje->ghie", weights_mix, value_rows, preferred_element_type=jnp.float32
    )
    inter_factor = jnp.exp(-head_decay[:, None] * (position[None, :] + 1.0))[:, :, None]
    inter_term = (
        jnp.einsum(
            "ghid,ghde->ghie",
            query,
            past_block.astype(jnp.bfloat16),
            preferred_element_type=jnp.float32,
        )
        * inter_factor
    )
    return intra_term + inter_term


def per_device(
    mesh_shape, tokens, past_states, attn_weights, ffn_weights, norm_gains, head_rates, end_lengths, new_slot
):
    sessions_here = end_lengths.shape[0]
    row_count = tokens.shape[0]
    event_count = row_count // sessions_here
    heads_here = past_states.shape[1]
    head_dim = past_states.shape[3]
    tensor_at = lax.axis_index("tensor")
    head_decay = lax.dynamic_slice_in_dim(head_rates, tensor_at * heads_here, heads_here)
    peer_count = lax.axis_size("dp")
    pair_cap = max(2, 2 * sessions_here // peer_count)
    slot_count = peer_count * pair_cap
    survive = end_lengths > event_count
    live_len = jnp.minimum(end_lengths, event_count)
    target_dev = new_slot // sessions_here
    local_slot = new_slot % sessions_here
    session_ids = jnp.arange(sessions_here, dtype=jnp.int32)
    earlier = (
        (target_dev[None, :] == target_dev[:, None])
        & survive[None, :]
        & (session_ids[None, :] < session_ids[:, None])
    )
    pair_rank = jnp.sum(earlier, axis=1)
    buffer_pos = target_dev * pair_cap + pair_rank
    matches = (buffer_pos[None, :] == jnp.arange(slot_count, dtype=jnp.int32)[:, None]) & survive[
        None, :
    ]
    source = jnp.sum(jnp.where(matches, session_ids[None, :], 0), axis=1)
    filled = jnp.any(matches, axis=1)
    label_at = jnp.sum(jnp.where(matches, local_slot[None, :], 0), axis=1)
    labels = jnp.where(filled, label_at, -1).reshape(peer_count, 1, pair_cap)
    labels = jnp.pad(labels, ((0, 0), (0, 7), (0, 128 - pair_cap)), constant_values=-1)
    weights_attn, weights_out, sent_labels = exchange(
        mesh_shape,
        0,
        (attn_weights, "relay", "dp", 1, (0, 4)),
        (attn_weights, "gather", "tensor", 1, (4, 5)),
        (labels.astype(jnp.int32), "scatter", "dp", 0, None),
    )
    sent_labels = sent_labels[:, 0, 0, :pair_cap]
    float_tokens = tokens.astype(jnp.float32)
    normed = rms_scale(float_tokens, norm_gains[0])
    projected = jnp.einsum(
        "nd,mde->mne", normed, weights_attn, preferred_element_type=jnp.float32
    )

    def split_heads(matrix):
        return matrix.reshape(sessions_here, event_count, heads_here, head_dim).transpose(
            0, 2, 1, 3
        )

    query = split_heads(projected[0].astype(jnp.bfloat16))
    key_rows = split_heads(projected[1].astype(jnp.bfloat16))
    value_rows = split_heads(projected[2].astype(jnp.bfloat16))
    gate_rows = projected[3]
    retained = retain_events(query, key_rows, value_rows, past_states, head_decay)
    updated = update_state(past_states, key_rows, value_rows, head_decay)
    packed = pick(updated, source, filled, jnp.bfloat16)
    row_mean = jnp.mean(retained, axis=-1, keepdims=True)
    centred = retained - row_mean
    row_var = jnp.mean(centred * centred, axis=-1, keepdims=True)
    normalised = centred * lax.rsqrt(row_var + 1e-05)
    merged = normalised.transpose(0, 2, 1, 3).reshape(row_count, heads_here * head_dim)
    gated = (jax.nn.silu(gate_rows) * merged).astype(jnp.bfloat16)
    gated_all, weights_out, weights_ffn = exchange(
        mesh_shape,
        1,
        (gated, "chain", "tensor", 1, None),
        (weights_out, "relay", "dp", 0, None),
        (ffn_weights, "relay", "dp", 1, None),
    )
    attended = jnp.einsum("nc,dc->nd", gated_all, weights_out, preferred_element_type=jnp.float32)
    residual = float_tokens + attended
    hidden_in = rms_scale(residual, norm_gains[1])
    activated = jax.nn.gelu(
        jnp.dot(hidden_in, weights_ffn[0], preferred_element_type=jnp.float32), approximate=True
    ).astype(jnp.bfloat16)
    ffn_partial = jnp.einsum(
        "nf,df->nd", activated, weights_ffn[1], preferred_element_type=jnp.float32
    )
    ffn_terms, received = exchange(
        mesh_shape,
        2,
        (ffn_partial.astype(jnp.bfloat16), "scatter", "tensor", 1, None),
        (packed, "scatter", "dp", 0, None),
    )
    ffn_share = jnp.sum(ffn_terms.astype(jnp.float32), axis=0)
    flattened = received.reshape(packed.shape)
    found_at = sent_labels.reshape(-1)[None, :] == session_ids[:, None]
    which_slot = jnp.sum(
        jnp.where(found_at, jnp.arange(slot_count, dtype=jnp.int32)[None, :], 0), axis=1
    )
    present = jnp.any(found_at, axis=1)
    moved_states = pick(flattened, which_slot, present, jnp.float32)
    col_count = ffn_share.shape[1]
    residual_here = lax.dynamic_slice_in_dim(residual, tensor_at * col_count, col_count, 1)
    keep_rows = (jnp.arange(event_count, dtype=jnp.int32)[None, :] < live_len[:, None]).reshape(-1)
    next_tokens = jnp.where(keep_rows[:, None], residual_here + ffn_share, 0.0).astype(jnp.bfloat16)
    return (next_tokens, moved_states)


def solution(mesh):
    placed = (
        P(("group", "dp"), None),
        P(("group", "dp"), "tensor", None, None),
        P(None, "dp", "tensor"),
        P(None, "dp", "tensor"),
        P(),
        P(),
        P(("group", "dp")),
        P(("group", "dp")),
    )
    return jax.shard_map(
        functools.partial(per_device, dict(mesh.shape)),
        mesh=mesh,
        in_specs=placed,
        out_specs=(P(("group", "dp"), "tensor"), P(("group", "dp"), "tensor", None, None)),
        check_vma=False,
    )
```

profile of v0, /device:TPU:1, one launch (start us, length us, event | category | flops | bytes accessed | tf_op | source)
XLA Modules:
  0.0 177.7 jit_solution(13134538782167723502)
XLA Ops:
  0.6 0.0 copy-start.10
  0.6 0.7 and_select_fusion
  1.3 0.7 broadcast_compare_fusion
  2.0 0.2 convert_reduce_fusion.1
  2.2 0.1 select_reduce_fusion.1
  2.3 0.1 fusion.67
  2.4 0.1 select_n.59
  2.5 0.0 copy-start.2
  2.5 1.1 copy-done.2
  3.6 19.3 %shard_map.95 = (bf16[4,1024,256]{2,1,0:T(8,128)(2,1)S(1)}, bf16[256,1024]{1,0:T(8,128)(2,1)S(1)}, s32[4,1,8,128]{3,2,1,0:T(8,128)S(1)}) custom-call(bf16[5,256,256]{2,1,0:T(8,128)(2,1)S(1)} %copy-done.2, bf16[5,256,256]{2,1,0:T(8,128)(2,1)S(1)} %copy-done.2, s32[4,8,128]{2,1,0:T(8,128)S(1)} %pad.4.refs_2_), custom_call_target="tpu_custom_call" | custom-call | bytes 10616832 | tf_op jit(solution)/shard_map/pallas_call | solution.py:244
  22.8 4.0 %copy.31 = bf16[1024,1024]{0,1:T(8,128)(2,1)} copy(bf16[1024,1024]{1,0:T(8,128)(2,1)} %param.8) | data formatting | bytes 4194304 | tf_op args[0]
  26.8 2.1 %fusion = f32[1024]{0:T(1024)S(1)} fusion(bf16[1024,1024]{0,1:T(8,128)(2,1)} %copy.31), kind=kLoop, calls=%fused_computation.4 | loop fusion | flops 3144704 | bytes 2101248 | tf_op jit(solution)/shard_map/reduce_sum | solution.py:258
  28.9 0.0 copy-done.10
  28.9 6.2 %fusion.75 = (bf16[4,1024,256]{2,1,0:T(8,128)(2,1)S(1)}, f32[4,1024,256]{2,1,0:T(8,128)}) fusion(bf16[4,1024,256]{2,1,0:T(8,128)(2,1)S(1)} %get-tuple-element.10, bf16[1024,1024]{0,1:T(8,128)(2,1)} %copy.31, f32[1024]{0:T(1024)S(1)} %bitcast.79, f32[1024]{0:T(1024)S(1)} %add_rsqrt_fusion.1), kind=kOutput, calls=%fused_computation.111 | convolution fusion | flops 2152726528 | bytes 10493952 | tf_op jit(solution)/shard_map/nd,mde->mne/dot_general | solution.py:346
  35.1 0.9 fusion.73
  36.0 0.1 convert_element_type.89
  36.1 0.0 copy-start.9
  36.1 0.0 copy-start.11
  36.1 3.1 %fusion.26 = f32[32,2,32,128]{3,2,1,0:T(8,128)S(1)} fusion(f32[32,2,128,128]{3,2,1,0:T(8,128)} %param.9, bf16[32,32,2,128]{3,2,1,0:T(2,128)(2,1)S(1)} %convert_element_type.89), kind=kOutput, calls=%fused_computation.33 | convolution fusion | flops 68157440 | bytes 5767168 | tf_op jit(solution)/shard_map/ghid,ghde->ghie/dot_general | solution.py:292
  39.2 1.2 convert_element_type.90
  40.4 0.9 convert_element_type.93
  41.3 0.0 copy-done.11
  41.3 0.1 multiply_exponential_fusion.2
  41.4 0.1 exponential_multiply_fusion
  41.5 0.1 subtract_maximum_fusion
  41.5 0.1 subtract_compare_fusion
  41.6 0.0 copy-done.9
  41.6 0.1 select_multiply_fusion
  41.7 2.0 %fusion.63 = (f32[32,2,32]{2,1,0:T(2,128)S(1)}, f32[32,2,32,128]{3,2,1,0:T(8,128)S(1)}) fusion(f32[32,2,32,128]{3,2,1,0:T(8,128)S(1)} %fusion.26, f32[2,32]{1,0:T(2,128)S(1)} %get-tuple-element.36, bf16[32,32,2,128]{3,2,1,0:T(2,128)(2,1)} %convert_element_type.93, f32[2,32,32]{2,1,0:T(8,128)S(1)} %select_multiply_fusion, ...), kind=kOutput, calls=%fused_computation.66 | convolution fusion | flops 34469888 | bytes 3686656 | tf_op jit(solution)/shard_map/ghij,ghje->ghie/dot_general | solution.py:287
  43.7 0.8 multiply_reduce_fusion.1
  44.5 0.0 copy-start.5
  44.6 0.1 multiply_exponential_fusion.1
  44.6 0.7 fusion.44
  45.4 0.0 copy-start.7
  45.4 0.8 copy.39
  46.2 1.5 fusion.41.refs_0_
  47.7 0.0 copy-done.5
  47.7 45.4 %shard_map.96 = (bf16[1024,1024]{1,0:T(8,128)(2,1)S(1)}, bf16[1024,1024]{1,0:T(8,128)(2,1)S(1)}, bf16[2,1024,1024]{2,1,0:T(8,128)(2,1)S(1)}) custom-call(bf16[1024,256]{1,0:T(8,128)(2,1)S(1)} %fusion.41.refs_0_, bf16[256,1024]{1,0:T(8,128)(2,1)S(1)} %get-tuple-element.11.refs_1_, bf16[2,256,1024]{2,1,0:T(8,128)(2,1)S(1)} %copy-done.5), custom_call_target="tpu_custom_call" | custom-call | bytes 16777216 | tf_op jit(solution)/shard_map/pallas_call | solution.py:244
  93.2 0.0 copy-start.6
  93.2 2.0 %copy-done.6 = bf16[2,1024,1024]{2,1,0:T(8,128)(2,1)} copy-done((bf16[2,1024,1024]{2,1,0:T(8,128)(2,1)}, bf16[2,1024,1024]{2,1,0:T(8,128)(2,1)S(1)}, u32[]{:S(2)}) %copy-start.6) | copy-done | bytes 4194328
  95.2 0.0 copy-done.7
  95.2 4.4 %multiply_reduce_fusion = (f32[1024]{0:T(1024)S(1)}, f32[1024,1024]{0,1:T(8,128)}) fusion(bf16[1024,1024]{1,0:T(8,128)(2,1)S(1)} %get-tuple-element.12, bf16[1024,1024]{1,0:T(8,128)(2,1)S(1)} %get-tuple-element.13, bf16[1024,1024]{0,1:T(8,128)(2,1)S(1)} %copy-done.7), kind=kOutput, calls=%fused_computation.18 | convolution fusion | flops 2151676928 | bytes 10489856 | tf_op jit(solution)/shard_map/nc,dc->nd/dot_general | solution.py:375
  99.5 8.7 %fusion.30.refs_0_ = bf16[1024,1024]{1,0:T(8,128)(2,1)S(1)} fusion(bf16[2,1024,1024]{2,1,0:T(8,128)(2,1)} %copy-done.6, f32[1024,1024]{0,1:T(8,128)} %get-tuple-element.44, f32[1024]{0:T(1024)S(1)} %bitcast.78, f32[1024]{0:T(1024)S(1)} %add_rsqrt_fusion), kind=kOutput, calls=%fused_computation.37 | convolution fusion | flops 4308598784 | bytes 10493952 | tf_op jit(solution)/shard_map/nf,df->nd/dot_general | solution.py:381
  108.3 0.0 copy-done.8
  108.3 5.1 %multiply_add_fusion.values_ref = f32[32,2,128,128]{3,2,1,0:T(8,128)} fusion(f32[32,2,128,128]{3,2,1,0:T(8,128)} %param.9, f32[2]{0:T(128)S(1)} %get-tuple-element.26, f32[2,32]{1,0:T(2,128)S(1)} %get-tuple-element.35, bf16[32,32,2,128]{3,2,1,0:T(2,128)(2,1)S(1)} %copy-done.8, bf16[32,32,2,128]{3,2,1,0:T(2,128)(2,1)S(1)} %convert_element_type.90), kind=kOutput, calls=%fused_computation.16 | convolution fusion | flops 69992448 | bytes 9437448 | tf_op jit(solution)/shard_map/ghjd,ghje->ghde/dot_general | solution.py:269
  113.4 3.4 %shard_map.97.refs_1_ = bf16[64,2,128,128]{3,2,1,0:T(8,128)(2,1)S(1)} custom-call(s32[64]{0:T(128)S(1)} %get-tuple-element.24.index_ref, s32[64]{0:T(128)S(1)} %convert_element_type.99.keep_ref, f32[32,2,128,128]{3,2,1,0:T(8,128)} %multiply_add_fusion.values_ref), custom_call_target="tpu_custom_call" | custom-call | tf_op jit(solution)/shard_map/pallas_call | solution.py:23
  116.8 48.5 %shard_map.98 = (bf16[4,1024,256]{2,1,0:T(8,128)(2,1)S(1)}, bf16[4,16,2,128,128]{4,3,2,1,0:T(8,128)(2,1)S(1)}) custom-call(bf16[1024,1024]{1,0:T(8,128)(2,1)S(1)} %fusion.30.refs_0_, bf16[64,2,128,128]{3,2,1,0:T(8,128)(2,1)S(1)} %shard_map.97.refs_1_), custom_call_target="tpu_custom_call" | custom-call | bytes 50331648 | tf_op jit(solution)/shard_map/pallas_call | solution.py:244
  165.4 0.0 copy-start
  165.4 2.0 %copy-done = bf16[4,16,2,128,128]{4,3,2,1,0:T(8,128)(2,1)} copy-done((bf16[4,16,2,128,128]{4,3,2,1,0:T(8,128)(2,1)}, bf16[4,16,2,128,128]{4,3,2,1,0:T(8,128)(2,1)S(1)}, u32[]{:S(2)}) %copy-start) | copy-done | bytes 4194328
  167.4 1.3 copy-done.3
  168.7 0.1 eq.49
  168.8 0.1 fusion.64
  168.9 0.1 select_reduce_fusion.index_ref
  169.0 0.0 copy-start.1
  169.1 2.2 %copy-done.1 = bf16[4,16,2,128,128]{4,3,2,1,0:T(8,128)(2,1)S(1)} copy-done((bf16[4,16,2,128,128]{4,3,2,1,0:T(8,128)(2,1)S(1)}, bf16[4,16,2,128,128]{4,3,2,1,0:T(8,128)(2,1)}, u32[]{:S(2)}) %copy-start.1) | copy-done | bytes 4194328
  171.2 3.1 %shard_map.99 = f32[32,2,128,128]{3,2,1,0:T(8,128)} custom-call(s32[32]{0:T(128)S(1)} %select_reduce_fusion.index_ref, s32[32]{0:T(128)S(1)} %convert_element_type.104.keep_ref, bf16[64,2,128,128]{3,2,1,0:T(8,128)(2,1)S(1)} %bitcast.75), custom_call_target="tpu_custom_call" | custom-call | tf_op jit(solution)/shard_map/pallas_call | solution.py:23
  174.3 0.0 copy-done.4
  174.3 0.3 convert_reduce_fusion
  174.7 0.3 copy.40
  175.0 0.0 copy-done.12
  175.0 0.1 iota_compare_fusion.3
  175.1 0.1 lt.48
  175.2 1.5 select_convert_fusion
  176.7 1.0 copy.41
  (18 shorter events, 0.1 us)
Async XLA Ops:
  0.6 28.2 %copy-start.10 = (f32[2,1024]{1,0:T(2,128)S(1)}, f32[2,1024]{1,0:T(2,128)}, u32[]{:S(2)}) copy-start(f32[2,1024]{1,0:T(2,128)} %param.12) | copy-start | bytes 24580
  2.5 1.1 copy-start.2
  36.1 5.5 %copy-start.9 = (bf16[32,32,2,128]{3,2,1,0:T(2,128)(2,1)}, bf16[32,32,2,128]{3,2,1,0:T(2,128)(2,1)S(1)}, u32[]{:S(2)}) copy-start(bf16[32,32,2,128]{3,2,1,0:T(2,128)(2,1)S(1)} %convert_element_type.89) | copy-start | bytes 1572868
  36.1 5.2 %copy-start.11 = (f32[8]{0:T(128)S(1)}, f32[8]{0:T(128)}, u32[]{:S(2)}) copy-start(f32[8]{0:T(128)} %param.13) | copy-start | bytes 100
  44.5 3.2 %copy-start.5 = (bf16[2,256,1024]{2,1,0:T(8,128)(2,1)S(1)}, bf16[2,256,1024]{2,1,0:T(8,128)(2,1)}, u32[]{:S(2)}) copy-start(bf16[2,256,1024]{2,1,0:T(8,128)(2,1)} %refs_2_.1) | copy-start | bytes 3145732
  45.4 49.8 %copy-start.7 = (bf16[1024,1024]{0,1:T(8,128)(2,1)S(1)}, bf16[1024,1024]{0,1:T(8,128)(2,1)}, u32[]{:S(2)}) copy-start(bf16[1024,1024]{0,1:T(8,128)(2,1)} %copy.31) | copy-start | bytes 6291460
  93.2 2.0 %copy-start.6 = (bf16[2,1024,1024]{2,1,0:T(8,128)(2,1)}, bf16[2,1024,1024]{2,1,0:T(8,128)(2,1)S(1)}, u32[]{:S(2)}) copy-start(bf16[2,1024,1024]{2,1,0:T(8,128)(2,1)S(1)} %get-tuple-element.14) | copy-start | bytes 12582916
  99.5 8.8 %copy-start.8 = (bf16[32,32,2,128]{3,2,1,0:T(2,128)(2,1)S(1)}, bf16[32,32,2,128]{3,2,1,0:T(2,128)(2,1)}, u32[]{:S(2)}) copy-start(bf16[32,32,2,128]{3,2,1,0:T(2,128)(2,1)} %convert_element_type.93) | copy-start | bytes 1572868
  165.4 2.0 %copy-start = (bf16[4,16,2,128,128]{4,3,2,1,0:T(8,128)(2,1)}, bf16[4,16,2,128,128]{4,3,2,1,0:T(8,128)(2,1)S(1)}, u32[]{:S(2)}) copy-start(bf16[4,16,2,128,128]{4,3,2,1,0:T(8,128)(2,1)S(1)} %get-tuple-element.17) | copy-start | bytes 12582916
  167.4 1.3 copy-start.3
  169.0 2.2 %copy-start.1 = (bf16[4,16,2,128,128]{4,3,2,1,0:T(8,128)(2,1)S(1)}, bf16[4,16,2,128,128]{4,3,2,1,0:T(8,128)(2,1)}, u32[]{:S(2)}) copy-start(bf16[4,16,2,128,128]{4,3,2,1,0:T(8,128)(2,1)} %copy-done) | copy-start | bytes 12582916
  171.2 3.1 %copy-start.4 = (bf16[4,1024,256]{2,1,0:T(8,128)(2,1)S(1)}, bf16[4,1024,256]{2,1,0:T(8,128)(2,1)}, u32[]{:S(2)}) copy-start(bf16[4,1024,256]{2,1,0:T(8,128)(2,1)} %copy-done.3) | copy-start | bytes 6291460
  174.3 0.7 copy-start.12
where the time goes:
time: 178 us
  Pallas kernels  120 us (67%)
  matrix products  29.4 us (17%)
  local copies, waits for them, and re-layouts  18.2 us (10%)
  other arithmetic  9.46 us (5%)
    pallas_call x3, Pallas kernels, exchange(): pl.pallas_call(functools.partial(exchange_kernel, tuple((task[1:] for tas...  113 us
    unnamed x28, local copies, waits for them, and re-layouts  13.6 us
    dot_general x1, matrix products, per_device(): jnp.einsum('nf,df->nd', activated, weights_ffn[1], preferred_element_type...  8.74 us
    pallas_call x2, Pallas kernels, pick(): pl.pallas_call(pick_kernel, out_shape=jax.ShapeDtypeStruct(index.shape +...  6.49 us
    dot_general x1, matrix products, per_device(): jnp.einsum('nd,mde->mne', normed, weights_attn, preferred_element_type=jn...  6.2 us
    dot_general x1, matrix products, update_state(): jnp.einsum('ghjd,ghje->ghde', weighted.astype(jnp.bfloat16), value_rows,...  5.09 us
    dot_general x1, matrix products, per_device(): jnp.einsum('nc,dc->nd', gated_all, weights_out, preferred_element_type=jn...  4.36 us

commit v1 on v0

--- a/solution.py
+++ b/solution.py
@@ -39,8 +39,11 @@
     return ref.at[tuple(index)]
 
 
-def exchange_kernel(jobs, axes, *refs):
+def exchange_kernel(jobs, axes, with_norm, *refs):
     count = len(jobs)
+    if with_norm:
+        (rows_ref, gain_ref), normed_ref = refs[count : count + 2], refs[2 * count + 2]
+        refs = refs[:count] + refs[count + 2 : 2 * count + 2] + refs[2 * count + 3 :]
     sources, outs = refs[:count], refs[count : 2 * count]
     sems, held = refs[2 * count : 3 * count], refs[3 * count :]
     barrier = pltpu.get_barrier_semaphore()
@@ -200,6 +203,15 @@
         fetch.wait()
         put.start()
         arrivals.append(put.wait)
+    if with_norm:
+        step_rows = min(64, rows_ref.shape[0])
+
+        def norm_step(at, carry):
+            rows = pl.ds(pl.multiple_of(at * step_rows, step_rows), step_rows)
+            normed_ref[rows] = rms_scale(rows_ref[rows].astype(jnp.float32), gain_ref[...])
+            return carry
+
+        lax.fori_loop(0, rows_ref.shape[0] // step_rows, norm_step, 0)
     for _, act in sorted(events, key=lambda event: event[0]):
         act()
     for wait in arrivals:
@@ -215,7 +227,7 @@
     return max(1, min(8, width // 16) // groups)
 
 
-def exchange(mesh_shape, collective_id, *tasks):
+def exchange(mesh_shape, collective_id, *tasks, norm=()):
     used = [task[2] for task in tasks] + ["group" for task in tasks if task[1] == "relay"]
     axes = tuple((axis, mesh_shape[axis]) for axis in ("group", "dp", "tensor") if axis in used)
     shapes, sems, held = [], [], []
@@ -240,18 +252,21 @@
             shape[dim] *= size
         shapes.append(jax.ShapeDtypeStruct(tuple(shape), values.dtype))
         sems.append(pltpu.SemaphoreType.DMA((2, number)))
+    in_vmem = [pl.BlockSpec(memory_space=pltpu.VMEM)]
+    if norm:
+        shapes.append(jax.ShapeDtypeStruct(norm[0].shape, jnp.bfloat16))
     sent = sum(values.size * values.dtype.itemsize for values, *_ in tasks)
     return pl.pallas_call(
-        functools.partial(exchange_kernel, tuple(task[1:] for task in tasks), axes),
+        functools.partial(exchange_kernel, tuple(task[1:] for task in tasks), axes, bool(norm)),
         out_shape=shapes,
-        in_specs=[pl.BlockSpec(memory_space=pl.ANY)] * len(tasks),
-        out_specs=[pl.BlockSpec(memory_space=pl.ANY)] * len(tasks),
+        in_specs=[pl.BlockSpec(memory_space=pl.ANY)] * len(tasks) + in_vmem * len(norm),
+        out_specs=[pl.BlockSpec(memory_space=pl.ANY)] * len(tasks) + in_vmem * bool(norm),
         scratch_shapes=sems + held,
         cost_estimate=pl.CostEstimate(flops=0, bytes_accessed=8 * sent, transcendentals=0),
         compiler_params=pltpu.CompilerParams(
             collective_id=collective_id, has_side_effects=True, vmem_limit_bytes=16 * 2**20
         ),
-    )(*(task[0] for task in tasks))
+    )(*(task[0] for task in tasks), *norm)
 
 
 def rms_scale(values, gain_row):
@@ -333,19 +348,20 @@
     label_at = jnp.sum(jnp.where(matches, local_slot[None, :], 0), axis=1)
     labels = jnp.where(filled, label_at, -1).reshape(peer_count, 1, pair_cap)
     labels = jnp.pad(labels, ((0, 0), (0, 7), (0, 128 - pair_cap)), constant_values=-1)
-    weights_attn, weights_out, sent_labels = exchange(
+    weights_attn, weights_out, sent_labels, normed = exchange(
         mesh_shape,
         0,
         (attn_weights, "relay", "dp", 1, (0, 4)),
         (attn_weights, "gather", "tensor", 1, (4, 5)),
         (labels.astype(jnp.int32), "scatter", "dp", 0, None),
+        norm=(tokens, norm_gains[:1]),
     )
     sent_labels = sent_labels[:, 0, 0, :pair_cap]
     float_tokens = tokens.astype(jnp.float32)
-    normed = rms_scale(float_tokens, norm_gains[0])
-    projected = jnp.einsum(
-        "nd,mde->mne", normed, weights_attn, preferred_element_type=jnp.float32
-    )
+    projected = [
+        jnp.dot(normed, weights_attn[which], preferred_element_type=jnp.float32)
+        for which in range(4)
+    ]
 
     def split_heads(matrix):
         return matrix.reshape(sessions_here, event_count, heads_here, head_dim).transpose(

time: 178 us -> 189 us (1.062)
  local copies, waits for them, and re-layouts: 18.2 us -> 24.9 us
  matrix products: 29.4 us -> 35.2 us
  other arithmetic: 9.46 us -> 7.44 us
    unnamed x28 -> x42, local copies, waits for them, and re-layouts: 13.6 us -> 18.3 us
    reshape x0 -> x3, local copies, waits for them, and re-layouts: none -> 4.32 us  [split_heads(): matrix.reshape(sessions_here, event_count, heads_here, head_dim)]
    dot_general x1, matrix products: 4.36 us -> 7.2 us  [per_device(): jnp.einsum('nc,dc->nd', gated_all, weights_out, preferred_element_type=jn...]
    convert_element_type x3 -> x0, local copies, waits for them, and re-layouts: 2.21 us -> none  [the longest x1 1.17 us: per_device(): key_rows = split_heads(projected[1].astype(jnp.bfloat16))]
    reduce_sum x1 -> x0, other arithmetic: 2.07 us -> none  [rms_scale(): meansq = jnp.mean(values * values, axis=-1, keepdims=True)]
    dot_general x1 -> x4, matrix products: 6.2 us -> 6.87 us  [per_device(): jnp.dot(normed, weights_attn[which], preferred_element_type=jnp.float32)]
where the time goes in v1:
time: 189 us; the launch traced here: 188 us
  Pallas kernels  120 us (63%)
  matrix products  35.2 us (19%)
  local copies, waits for them, and re-layouts  24.9 us (13%)
  other arithmetic  7.44 us (4%)
    pallas_call x3, Pallas kernels, exchange(): pl.pallas_call(functools.partial(exchange_kernel, tuple((task[1:] for tas...  113 us
    unnamed x42, local copies, waits for them, and re-layouts  18.3 us
    dot_general x1, matrix products, per_device(): jnp.einsum('nf,df->nd', activated, weights_ffn[1], preferred_element_type...  8.77 us
    dot_general x1, matrix products, per_device(): jnp.einsum('nc,dc->nd', gated_all, weights_out, preferred_element_type=jn...  7.2 us
    dot_general x4, matrix products, per_device(): jnp.dot(normed, weights_attn[which], preferred_element_type=jnp.float32)  6.87 us
    pallas_call x2, Pallas kernels, pick(): pl.pallas_call(pick_kernel, out_shape=jax.ShapeDtypeStruct(index.shape +...  6.49 us
    dot_general x1, matrix products, update_state(): jnp.einsum('ghjd,ghje->ghde', weighted.astype(jnp.bfloat16), value_rows,...  5.09 us
    reshape x3, local copies, waits for them, and re-layouts, split_heads(): matrix.reshape(sessions_here, event_count, heads_here, head_dim)  4.32 us

profile of v1, /device:TPU:1, one launch (start us, length us, event | category | flops | bytes accessed | tf_op | source)
XLA Modules:
  0.0 187.9 jit_solution(3966000440997381526)
XLA Ops:
  0.6 0.7 and_select_fusion
  1.3 0.7 broadcast_compare_fusion
  2.0 0.2 convert_reduce_fusion.1
  2.1 0.1 select_reduce_fusion.1
  2.2 0.1 fusion.71
  2.4 0.1 select_n.59
  2.4 0.8 fusion.77
  3.2 0.0 copy-start
  3.2 1.6 copy-done
  4.8 1.1 copy-done.4
  5.9 19.3 %shard_map.95 = (bf16[4,1024,256]{2,1,0:T(8,128)(2,1)S(1)}, bf16[256,1024]{1,0:T(8,128)(2,1)S(1)}, s32[4,1,8,128]{3,2,1,0:T(8,128)S(1)}, bf16[1024,1024]{1,0:T(8,128)(2,1)S(1)}) custom-call(bf16[5,256,256]{2,1,0:T(8,128)(2,1)S(1)} %copy-done.4, bf16[5,256,256]{2,1,0:T(8,128)(2,1)S(1)} %copy-done.4, s32[4,8,128]{2,1,0:T(8,128)S(1)} %pad.4.refs_2_, ...), custom_call_target="tpu_custom_call" | custom-call | bytes 10616832 | tf_op jit(solution)/shard_map/pallas_call | solution.py:259
  25.2 0.0 copy-start.9
  25.2 1.3 copy-done.9
  26.5 1.5 convolution_convert_fusion.2
  28.0 1.2 reshape.190
  29.2 0.0 copy-start.10
  29.2 4.1 %fusion.21 = f32[32,2,32,128]{3,2,1,0:T(8,128)} fusion(f32[32,2,128,128]{3,2,1,0:T(8,128)} %param.9, bf16[32,32,2,128]{3,2,1,0:T(2,128)(2,1)S(1)} %reshape.190), kind=kOutput, calls=%fused_computation.26 | convolution fusion | flops 68157440 | bytes 5767168 | tf_op jit(solution)/shard_map/ghid,ghde->ghie/dot_general | solution.py:307
  33.3 0.0 copy-done.10
  33.3 1.5 convolution_convert_fusion.1
  34.8 1.2 reshape.191
  36.0 0.0 copy-start.18
  36.0 3.1 %convolution_convert_fusion = bf16[1024,256]{1,0:T(8,128)(2,1)} fusion(bf16[1024,1024]{1,0:T(8,128)(2,1)} %copy-done.9, bf16[4,1024,256]{2,1,0:T(8,128)(2,1)S(1)} %get-tuple-element.12), kind=kOutput, calls=%fused_computation.30 | convolution fusion | flops 537133056 | bytes 3145728 | tf_op jit(solution)/shard_map/dot_general | solution.py:362
  39.1 2.0 %reshape.192 = bf16[32,32,2,128]{3,2,1,0:T(2,128)(2,1)} reshape(bf16[1024,256]{1,0:T(8,128)(2,1)} %convolution_convert_fusion) | data formatting | bytes 1048576 | tf_op jit(solution)/shard_map/reshape | solution.py:367
  41.1 0.1 multiply_exponential_fusion.2
  41.2 0.1 exponential_multiply_fusion
  41.2 0.1 subtract_maximum_fusion
  41.3 0.1 subtract_compare_fusion
  41.4 0.1 select_multiply_fusion
  41.5 3.2 %fusion.67 = (f32[32,2,32]{2,1,0:T(2,128)S(1)}, f32[32,2,32,128]{3,2,1,0:T(8,128)}) fusion(f32[32,2,32,128]{3,2,1,0:T(8,128)} %fusion.21, f32[2,32]{1,0:T(2,128)S(1)} %get-tuple-element.35, bf16[32,32,2,128]{3,2,1,0:T(2,128)(2,1)} %reshape.192, f32[2,32,32]{2,1,0:T(8,128)S(1)} %select_multiply_fusion, bf16[32,32,2,128]{3,2,1,0:T(2,128)(2,1)S(1)} %reshape.191, ...), kind=kOutput, calls=%fused_computation.68 | convolution fusion | flops 34469888 | bytes 3686656 | tf_op jit(solution)/shard_map/ghij,ghje->ghie/dot_general | solution.py:302
  44.7 0.0 copy-start.14
  44.7 2.3 %multiply_reduce_fusion.1 = f32[32,2,32]{2,1,0:T(2,128)S(1)} fusion(f32[32,2,32]{2,1,0:T(2,128)S(1)} %get-tuple-element.31, f32[32,2,32,128]{3,2,1,0:T(8,128)} %get-tuple-element.39, f32[32,2,32,128]{3,2,1,0:T(8,128)} %fusion.21, f32[2,32]{1,0:T(2,128)S(1)} %get-tuple-element.35), kind=kLoop, calls=%fused_computation.43 | loop fusion | flops 1308672 | bytes 2113792 | tf_op jit(solution)/shard_map/reduce_sum | solution.py:380
  47.1 0.1 multiply_exponential_fusion.1
  47.2 0.7 fusion.37
  47.9 0.8 copy.30
  48.8 0.0 copy-done.11
  48.8 0.8 fusion.34.refs_0_
  49.5 0.0 copy-start.1
  49.6 0.4 copy-done.7
  50.0 45.3 %shard_map.96 = (bf16[1024,1024]{1,0:T(8,128)(2,1)S(1)}, bf16[1024,1024]{1,0:T(8,128)(2,1)S(1)}, bf16[2,1024,1024]{2,1,0:T(8,128)(2,1)S(1)}) custom-call(bf16[1024,256]{1,0:T(8,128)(2,1)S(1)} %fusion.34.refs_0_, bf16[256,1024]{1,0:T(8,128)(2,1)S(1)} %get-tuple-element.13.refs_1_, bf16[2,256,1024]{2,1,0:T(8,128)(2,1)S(1)} %copy-done.7), custom_call_target="tpu_custom_call" | custom-call | bytes 16777216 | tf_op jit(solution)/shard_map/pallas_call | solution.py:259
  95.3 0.0 copy-start.8
  95.3 2.0 %copy-done.8 = bf16[2,1024,1024]{2,1,0:T(8,128)(2,1)} copy-done((bf16[2,1024,1024]{2,1,0:T(8,128)(2,1)}, bf16[2,1024,1024]{2,1,0:T(8,128)(2,1)S(1)}, u32[]{:S(2)}) %copy-start.8) | copy-done | bytes 4194328
  97.3 1.3 copy-done.12
  98.7 1.3 copy-done.13
  100.0 2.6 %copy.25 = bf16[1024,1024]{0,1:T(8,128)(2,1)} copy(bf16[1024,1024]{1,0:T(8,128)(2,1)S(1)} %copy-done.1) | data formatting | bytes 4194304 | tf_op args[0]
  102.6 7.2 %multiply_reduce_fusion = (f32[1024]{0:T(1024)S(1)}, f32[1024,1024]{0,1:T(8,128)}) fusion(bf16[1024,1024]{1,0:T(8,128)(2,1)} %copy-done.12, bf16[1024,1024]{1,0:T(8,128)(2,1)} %copy-done.13, bf16[1024,1024]{0,1:T(8,128)(2,1)} %copy.25), kind=kOutput, calls=%fused_computation.12 | convolution fusion | flops 2151676928 | bytes 10489856 | tf_op jit(solution)/shard_map/nc,dc->nd/dot_general | solution.py:391
  109.8 8.8 %fusion.23.refs_0_ = bf16[1024,1024]{1,0:T(8,128)(2,1)S(1)} fusion(bf16[2,1024,1024]{2,1,0:T(8,128)(2,1)} %copy-done.8, f32[1024,1024]{0,1:T(8,128)} %get-tuple-element.41, f32[1024]{0:T(1024)S(1)} %bitcast.83, f32[1024]{0:T(1024)S(1)} %add_rsqrt_fusion), kind=kOutput, calls=%fused_computation.28 | convolution fusion | flops 4308598784 | bytes 10493952 | tf_op jit(solution)/shard_map/nf,df->nd/dot_general | solution.py:397
  118.6 5.1 %multiply_add_fusion.values_ref = f32[32,2,128,128]{3,2,1,0:T(8,128)} fusion(f32[32,2,128,128]{3,2,1,0:T(8,128)} %param.9, f32[2]{0:T(128)S(1)} %get-tuple-element.28, f32[2,32]{1,0:T(2,128)S(1)} %get-tuple-element.34, bf16[32,32,2,128]{3,2,1,0:T(2,128)(2,1)S(1)} %copy-done.16, bf16[32,32,2,128]{3,2,1,0:T(2,128)(2,1)S(1)} %reshape.191), kind=kOutput, calls=%fused_computation.10 | convolution fusion | flops 69992448 | bytes 9437448 | tf_op jit(solution)/shard_map/ghjd,ghje->ghde/dot_general | solution.py:284
  123.7 3.4 %shard_map.97.refs_1_ = bf16[64,2,128,128]{3,2,1,0:T(8,128)(2,1)S(1)} custom-call(s32[64]{0:T(128)S(1)} %get-tuple-element.26.index_ref, s32[64]{0:T(128)S(1)} %convert_element_type.89.keep_ref, f32[32,2,128,128]{3,2,1,0:T(8,128)} %multiply_add_fusion.values_ref), custom_call_target="tpu_custom_call" | custom-call | tf_op jit(solution)/shard_map/pallas_call | solution.py:23
  127.1 48.5 %shard_map.98 = (bf16[4,1024,256]{2,1,0:T(8,128)(2,1)S(1)}, bf16[4,16,2,128,128]{4,3,2,1,0:T(8,128)(2,1)S(1)}) custom-call(bf16[1024,1024]{1,0:T(8,128)(2,1)S(1)} %fusion.23.refs_0_, bf16[64,2,128,128]{3,2,1,0:T(8,128)(2,1)S(1)} %shard_map.97.refs_1_), custom_call_target="tpu_custom_call" | custom-call | bytes 50331648 | tf_op jit(solution)/shard_map/pallas_call | solution.py:259
  175.6 0.0 copy-start.2
  175.6 2.0 %copy-done.2 = bf16[4,16,2,128,128]{4,3,2,1,0:T(8,128)(2,1)} copy-done((bf16[4,16,2,128,128]{4,3,2,1,0:T(8,128)(2,1)}, bf16[4,16,2,128,128]{4,3,2,1,0:T(8,128)(2,1)S(1)}, u32[]{:S(2)}) %copy-start.2) | copy-done | bytes 4194328
  177.6 1.3 copy-done.5
  179.0 0.1 eq.49
  179.1 0.1 fusion.68
  179.2 0.1 select_reduce_fusion.index_ref
  179.3 0.0 copy-start.3
  179.3 2.2 %copy-done.3 = bf16[4,16,2,128,128]{4,3,2,1,0:T(8,128)(2,1)S(1)} copy-done((bf16[4,16,2,128,128]{4,3,2,1,0:T(8,128)(2,1)S(1)}, bf16[4,16,2,128,128]{4,3,2,1,0:T(8,128)(2,1)}, u32[]{:S(2)}) %copy-start.3) | copy-done | bytes 4194328
  181.5 3.1 %shard_map.99 = f32[32,2,128,128]{3,2,1,0:T(8,128)} custom-call(s32[32]{0:T(128)S(1)} %select_reduce_fusion.index_ref, s32[32]{0:T(128)S(1)} %convert_element_type.94.keep_ref, bf16[64,2,128,128]{3,2,1,0:T(8,128)(2,1)S(1)} %bitcast.80), custom_call_target="tpu_custom_call" | custom-call | tf_op jit(solution)/shard_map/pallas_call | solution.py:23
  184.6 0.3 convert_reduce_fusion
  184.9 0.3 copy.31
  185.3 0.1 iota_compare_fusion.3
  185.4 0.1 lt.48
  185.4 1.5 select_convert_fusion
  186.9 1.0 copy.32
  (31 shorter events, 0.2 us)
Async XLA Ops:
  3.2 1.6 copy-start
  4.8 1.1 copy-start.4
  25.2 1.3 copy-start.9
  29.2 4.1 %copy-start.17 = (bf16[32,32,2,128]{3,2,1,0:T(2,128)(2,1)}, bf16[32,32,2,128]{3,2,1,0:T(2,128)(2,1)S(1)}, u32[]{:S(2)}) copy-start(bf16[32,32,2,128]{3,2,1,0:T(2,128)(2,1)S(1)} %reshape.190) | copy-start | bytes 1572868
  29.2 4.1 %copy-start.10 = (bf16[1024,1024]{1,0:T(8,128)(2,1)S(1)}, bf16[1024,1024]{1,0:T(8,128)(2,1)}, u32[]{:S(2)}) copy-start(bf16[1024,1024]{1,0:T(8,128)(2,1)} %copy-done.9) | copy-start | bytes 6291460
  36.0 5.1 %copy-start.18 = (f32[8]{0:T(128)S(1)}, f32[8]{0:T(128)}, u32[]{:S(2)}) copy-start(f32[8]{0:T(128)} %param.13) | copy-start | bytes 100
  44.7 2.5 %copy-start.14 = (f32[32,2,32,128]{3,2,1,0:T(8,128)S(1)}, f32[32,2,32,128]{3,2,1,0:T(8,128)}, u32[]{:S(2)}) copy-start(f32[32,2,32,128]{3,2,1,0:T(8,128)} %fusion.21) | copy-start | bytes 3145732
  44.7 2.5 %copy-start.15 = (f32[32,2,32,128]{3,2,1,0:T(8,128)S(1)}, f32[32,2,32,128]{3,2,1,0:T(8,128)}, u32[]{:S(2)}) copy-start(f32[32,2,32,128]{3,2,1,0:T(8,128)} %get-tuple-element.39) | copy-start | bytes 3145732
  47.2 1.6 copy-start.11
  48.8 1.2 copy-start.7
  49.5 50.5 %copy-start.1 = (bf16[1024,1024]{1,0:T(8,128)(2,1)S(1)}, bf16[1024,1024]{1,0:T(8,128)(2,1)}, u32[]{:S(2)}) copy-start(bf16[1024,1024]{1,0:T(8,128)(2,1)} %refs_3_.1) | copy-start | bytes 6291460
  95.3 2.0 %copy-start.8 = (bf16[2,1024,1024]{2,1,0:T(8,128)(2,1)}, bf16[2,1024,1024]{2,1,0:T(8,128)(2,1)S(1)}, u32[]{:S(2)}) copy-start(bf16[2,1024,1024]{2,1,0:T(8,128)(2,1)S(1)} %get-tuple-element.16) | copy-start | bytes 12582916
  97.3 1.3 copy-start.12
  98.7 1.3 copy-start.13
  109.8 8.8 %copy-start.16 = (bf16[32,32,2,128]{3,2,1,0:T(2,128)(2,1)S(1)}, bf16[32,32,2,128]{3,2,1,0:T(2,128)(2,1)}, u32[]{:S(2)}) copy-start(bf16[32,32,2,128]{3,2,1,0:T(2,128)(2,1)} %reshape.192) | copy-start | bytes 1572868
  175.6 2.0 %copy-start.2 = (bf16[4,16,2,128,128]{4,3,2,1,0:T(8,128)(2,1)}, bf16[4,16,2,128,128]{4,3,2,1,0:T(8,128)(2,1)S(1)}, u32[]{:S(2)}) copy-start(bf16[4,16,2,128,128]{4,3,2,1,0:T(8,128)(2,1)S(1)} %get-tuple-element.19) | copy-start | bytes 12582916
  177.6 1.3 copy-start.5
  179.3 2.2 %copy-start.3 = (bf16[4,16,2,128,128]{4,3,2,1,0:T(8,128)(2,1)S(1)}, bf16[4,16,2,128,128]{4,3,2,1,0:T(8,128)(2,1)}, u32[]{:S(2)}) copy-start(bf16[4,16,2,128,128]{4,3,2,1,0:T(8,128)(2,1)} %copy-done.2) | copy-start | bytes 12582916
  181.5 3.1 %copy-start.6 = (bf16[4,1024,256]{2,1,0:T(8,128)(2,1)S(1)}, bf16[4,1024,256]{2,1,0:T(8,128)(2,1)}, u32[]{:S(2)}) copy-start(bf16[4,1024,256]{2,1,0:T(8,128)(2,1)} %copy-done.5) | copy-start | bytes 6291460
  184.6 0.7 copy-start.19
